TPU v7x, 32 devices: a whole 2x2x4 slice. The times are simulated.
32 devices in a mesh: groups: 2 (over x), tp: 4 (over y, core), dp: 4 (over z).
Axes of the slice: x: 2, y: 2, z: 4, core: 2. Of those that a mesh axis runs over, the one named last changes fastest.
Arguments:
- filter_feed_series: bfloat16 [4, 64, 8192], P(None, ('groups', 'dp'), 'tp'), parts along dimension 1, may hold values from -6 to 6
- valve_branch_series: bfloat16 [4, 64, 8192], P(None, ('groups', 'dp'), 'tp'), parts along dimension 1, may hold values from -6 to 6
- raw_increment_entries: bfloat16 [4, 64, 8192], P(None, ('groups', 'dp'), 'tp'), parts along dimension 1, may hold values from -6 to 6
- entering_memory_matrix: float32 [4, 64, 16], P(None, ('groups', 'dp')), parts along dimension 1, may hold values from -6 to 6
- leaving_memory_matrix: float32 [4, 64, 16], P(None, ('groups', 'dp')), parts along dimension 1, may hold values from -6 to 6
- emission_matrix: bfloat16 [8192, 4096], P('tp'), may hold values from -0.0625 to 0.0625
- recurrent_memory: float32 [8192, 1024], P('tp', ('groups', 'dp')), parts along dimension 1, may hold values from -6 to 6
- filter_recent_history: float32 [8192, 256], P('tp', ('groups', 'dp')), parts along dimension 1, may hold values from -6 to 6
- logarithmic_fading_speeds: float32 [8192, 16], replicated, may hold values from -2 to 2.7
- filter_coefficients: float32 [8192, 4], replicated, may hold values from -3 to 3
- filter_offset_term: float32 [8192], replicated, may hold values from -1 to 1
- increment_offset_term: float32 [8192], replicated, may hold values from -3 to 0.5
- residual_factor: float32 [8192], replicated, may hold values from 0.5 to 1.5
- remaining_ranks: int32 [3], replicated, may hold values from 0 to 3, as said below
- holder_segment_tallies: int32 [3], replicated, may hold values from 1 to 23, 64 in all
Outputs:
- decoded: bfloat16 [4, 64, 4096], P(None, ('groups', 'dp')), parts along dimension 1
- relocated_emission_matrix: bfloat16 [23552, 4096], P(('groups', 'tp')), parts along dimension 0
- relocated_recurrent_memory: float32 [11776, 1024], P('tp', ('groups', 'dp')), parts along dimension 1
- relocated_filter_history: float32 [11776, 256], P('tp', ('groups', 'dp')), parts along dimension 1
There are 2 independent parts, one for each index of `groups`. A program takes and returns all parts, laid end to end along the dimension named above; an argument that names none is the same for every part. Nothing has to cross between parts.
Inputs may be any that keep to these rules, and one draw needn't show every extreme that they name: `remaining_ranks`: 3 distinct tp indices in increasing order; the first and the last index of tp are always among them. `holder_segment_tallies`: sums to 64; some owner has exactly 23 blocks.
All inputs are finite; a program needn't handle non-finite values.
Results may differ from a plain program's by a relative error of at most 0.008.
Values may be sent and summed in bfloat16 or wider, within the bound.
No kernel may reach another device: no remote copies, remote signals or barrier semaphores. Data moves between devices by JAX's collectives and lax.ppermute only.
A program may use at most 192 MiB of HBM per device.

v0:
```python
import jax
import jax.numpy as jnp
from jax import lax
from jax.sharding import PartitionSpec as P

BLOCK = 128


def lane_holder_assignment(remaining_ranks, holder_segment_tallies, holder_ranks):
    starts = jnp.cumsum(holder_segment_tallies) - holder_segment_tallies
    accelerator_roster = jnp.arange(holder_ranks, dtype=jnp.int32)
    corresponding_holder = (remaining_ranks[None, :] == accelerator_roster[:, None]).astype(
        jnp.int32
    )
    accelerator_first_lane = jnp.sum(corresponding_holder * starts[None, :], axis=1)
    accelerator_total = jnp.sum(corresponding_holder * holder_segment_tallies[None, :], axis=1)
    return (accelerator_first_lane, accelerator_total)


def pack_rows(columns, accelerator_first_lane, accelerator_total, slot_rows):
    padded = jnp.pad(columns, ((0, slot_rows), (0, 0)))
    places = jnp.arange(slot_rows, dtype=jnp.int32)

    def one_owner(start, count):
        rows = lax.dynamic_slice_in_dim(padded, start * BLOCK, slot_rows, 0)
        return jnp.where((places < count * BLOCK)[:, None], rows, jnp.zeros_like(rows))

    packed = jax.vmap(one_owner)(accelerator_first_lane, accelerator_total)
    return packed.reshape(-1, columns.shape[1])


def move_states(ssm_rows, conv_rows, accelerator_first_lane, accelerator_total, slot_rows):
    spread = (
        lax.all_to_all(ssm_rows, "tp", split_axis=1, concat_axis=0, tiled=True),
        lax.all_to_all(conv_rows, "tp", split_axis=1, concat_axis=0, tiled=True),
    )
    packed_ssm = pack_rows(spread[0], accelerator_first_lane, accelerator_total, slot_rows)
    packed_conv = pack_rows(spread[1], accelerator_first_lane, accelerator_total, slot_rows)
    landed = (
        lax.all_to_all(packed_ssm, "tp", split_axis=0, concat_axis=1, tiled=True),
        lax.all_to_all(packed_conv, "tp", split_axis=0, concat_axis=1, tiled=True),
    )
    return (landed[0], landed[1])


def take_rows(holder_directory, start, count, slot_rows):
    padded = jnp.pad(holder_directory, [(0, slot_rows)] + [(0, 0)] * (holder_directory.ndim - 1))
    return lax.dynamic_slice_in_dim(padded, start, count, 0)


def decode_steps(
    x_rows,
    z_rows,
    dt_rows,
    entering_memory_matrix,
    leaving_memory_matrix,
    ssm_rows,
    conv_rows,
    decay,
    taps,
    tap_bias,
    step_bias,
    skip_gain,
    weights,
):
    channels, steps, seqs = x_rows.shape
    latent_entries = ssm_rows.reshape(channels, seqs, -1)
    filter_recent_frame = conv_rows.reshape(channels, seqs, 4)
    results = []
    for step in range(steps):
        x_now = x_rows[:, step, :].astype(jnp.float32)
        filter_recent_frame = jnp.concatenate(
            [filter_recent_frame[:, :, 1:], x_now[:, :, None]], axis=2
        )
        inner = jax.nn.silu(
            jnp.sum(filter_recent_frame * taps[:, None, :], axis=2) + tap_bias[:, None]
        )
        delta = jax.nn.softplus(dt_rows[:, step, :].astype(jnp.float32) + step_bias[:, None])
        latent_entries = (
            jnp.exp(delta[:, :, None] * decay[:, None, :]) * latent_entries
            + (delta * inner)[:, :, None] * entering_memory_matrix[step][None, :, :]
        )
        output_y = (
            jnp.sum(latent_entries * leaving_memory_matrix[step][None, :, :], axis=2)
            + skip_gain[:, None] * inner
        )
        gated = (output_y * jax.nn.silu(z_rows[:, step, :].astype(jnp.float32))).astype(
            jnp.bfloat16
        )
        partial_out = lax.dot_general(
            gated, weights, (((0,), (0,)), ((), ())), preferred_element_type=jnp.float32
        )
        results.append(lax.psum(partial_out, "tp").astype(jnp.bfloat16))
    decoded = jnp.stack(results, axis=0)
    return (
        decoded,
        latent_entries.reshape(channels, -1),
        filter_recent_frame.reshape(channels, -1),
    )


def per_device(
    filter_feed_series,
    valve_branch_series,
    raw_increment_entries,
    entering_memory_matrix,
    leaving_memory_matrix,
    emission_matrix,
    recurrent_memory,
    filter_recent_history,
    logarithmic_fading_speeds,
    filter_coefficients,
    filter_offset_term,
    increment_offset_term,
    residual_factor,
    remaining_ranks,
    holder_segment_tallies,
):
    holder_ranks = lax.axis_size("tp")
    mine = lax.axis_index("tp")
    width = logarithmic_fading_speeds.shape[0]
    old_rows = emission_matrix.shape[0]
    fresh = holder_ranks * 3 // 4
    slot_rows = (width // BLOCK // fresh + 2) * BLOCK
    accelerator_first_lane, accelerator_total = lane_holder_assignment(
        remaining_ranks, holder_segment_tallies, holder_ranks
    )
    decay_all = -jnp.exp(logarithmic_fading_speeds)
    spread_w = lax.all_to_all(emission_matrix, "tp", split_axis=1, concat_axis=0, tiled=True)
    relocated_emission_matrix = lax.all_to_all(
        pack_rows(spread_w, accelerator_first_lane, accelerator_total, slot_rows),
        "tp",
        split_axis=0,
        concat_axis=1,
        tiled=True,
    )
    new_start = accelerator_first_lane[mine] * BLOCK
    keep_rows = (jnp.arange(slot_rows, dtype=jnp.int32) < accelerator_total[mine] * BLOCK)[:, None]
    start_ssm, start_conv = move_states(
        recurrent_memory,
        filter_recent_history,
        accelerator_first_lane,
        accelerator_total,
        slot_rows,
    )
    steps, seqs = (filter_feed_series.shape[0], filter_feed_series.shape[1])
    flat_x = jnp.transpose(filter_feed_series, (2, 0, 1)).reshape(old_rows, steps * seqs)
    flat_z = jnp.transpose(valve_branch_series, (2, 0, 1)).reshape(old_rows, steps * seqs)
    flat_dt = jnp.transpose(raw_increment_entries, (2, 0, 1)).reshape(old_rows, steps * seqs)
    spread_s = (
        lax.all_to_all(flat_x, "tp", split_axis=1, concat_axis=0, tiled=True),
        lax.all_to_all(flat_z, "tp", split_axis=1, concat_axis=0, tiled=True),
        lax.all_to_all(flat_dt, "tp", split_axis=1, concat_axis=0, tiled=True),
    )
    packed_x = pack_rows(spread_s[0], accelerator_first_lane, accelerator_total, slot_rows)
    packed_z = pack_rows(spread_s[1], accelerator_first_lane, accelerator_total, slot_rows)
    packed_dt = pack_rows(spread_s[2], accelerator_first_lane, accelerator_total, slot_rows)
    landed_s = (
        lax.all_to_all(packed_x, "tp", split_axis=0, concat_axis=1, tiled=True),
        lax.all_to_all(packed_z, "tp", split_axis=0, concat_axis=1, tiled=True),
        lax.all_to_all(packed_dt, "tp", split_axis=0, concat_axis=1, tiled=True),
    )
    x_rows = landed_s[0].reshape(slot_rows, steps, seqs)
    z_rows = landed_s[1].reshape(slot_rows, steps, seqs)
    dt_rows = landed_s[2].reshape(slot_rows, steps, seqs)
    decoded, final_ssm, final_conv = decode_steps(
        x_rows,
        z_rows,
        dt_rows,
        entering_memory_matrix,
        leaving_memory_matrix,
        start_ssm,
        start_conv,
        take_rows(decay_all, new_start, slot_rows, slot_rows),
        take_rows(filter_coefficients, new_start, slot_rows, slot_rows),
        take_rows(filter_offset_term, new_start, slot_rows, slot_rows),
        take_rows(increment_offset_term, new_start, slot_rows, slot_rows),
        take_rows(residual_factor, new_start, slot_rows, slot_rows),
        relocated_emission_matrix,
    )
    relocated_recurrent_memory = jnp.where(keep_rows, final_ssm, jnp.zeros_like(final_ssm))
    relocated_filter_history = jnp.where(keep_rows, final_conv, jnp.zeros_like(final_conv))
    return (
        decoded,
        relocated_emission_matrix,
        relocated_recurrent_memory,
        relocated_filter_history,
    )


def solution(mesh):
    placed = (
        P(None, ("groups", "dp"), "tp"),
        P(None, ("groups", "dp"), "tp"),
        P(None, ("groups", "dp"), "tp"),
        P(None, ("groups", "dp"), None),
        P(None, ("groups", "dp"), None),
        P("tp", None),
        P("tp", ("groups", "dp")),
        P("tp", ("groups", "dp")),
        P(),
        P(),
        P(),
        P(),
        P(),
        P(),
        P(),
    )
    return jax.shard_map(
        per_device,
        mesh=mesh,
        in_specs=placed,
        out_specs=(
            P(None, ("groups", "dp"), None),
            P(("groups", "tp"), None),
            P("tp", ("groups", "dp")),
            P("tp", ("groups", "dp")),
        ),
        check_vma=False,
    )
```

profile of v0, /device:TPU:1, one launch (start us, length us, event | category | flops | bytes accessed | tf_op | source)
XLA Modules:
  0.0 687.0 jit_solution(11918465486972389657)
XLA Ops:
  8.5 4.3 all-to-all-start.6
  12.9 5.4 while.16
  21.7 5.4 while.15
  30.7 5.4 while.12
  44.7 4.4 all-to-all-start.2
  49.1 13.8 %copy.92 = bf16[256,4,8,1024]{3,2,0,1:T(8,128)(2,1)} copy(bf16[256,4,8,1024]{3,2,1,0:T(8,128)(2,1)} %bitcast.315) | data formatting | bytes 33554432 | tf_op jit(solution)/shard_map/all_to_all | solution.py:129
  62.9 7.6 %all-to-all-start.10 = ((bf16[2048,4,1024]{2,0,1:T(8,128)(2,1)}), bf16[2048,4,1024]{2,0,1:T(8,128)(2,1)}, u32[]{:S(2)}, u32[]{:S(2)}) async-start(bf16[2048,4,1024]{2,0,1:T(8,128)(2,1)} %bitcast.314), calls=%async_computation.10 | async-start | bytes 33554432 | tf_op jit(solution)/shard_map/all_to_all | solution.py:129
  70.6 5.4 while.14
  76.9 12.4 %while.13 = (s32[]{:T(128)}, f32[11136,32]{0,1:T(8,128)S(1)}, s32[4,2]{0,1:T(2,128)S(1)}, f32[4,2944,32]{1,2,0:T(8,128)}) while((s32[]{:T(128)}, f32[11136,32]{0,1:T(8,128)S(1)}, s32[4,2]{0,1:T(2,128)S(1)}, f32[4,2944,32]{1,2,0:T(8,128)}) %tuple.154), condition=%wide.while_cond.1.clone, body=%wide.while_body.1.sunk.clone | while | flops 2 | bytes 3014753 | solution.py:25
  89.3 163.5 %all-to-all-done.10 = bf16[2048,4,1024]{2,0,1:T(8,128)(2,1)} async-done(((bf16[2048,4,1024]{2,0,1:T(8,128)(2,1)}), bf16[2048,4,1024]{2,0,1:T(8,128)(2,1)}, u32[]{:S(2)}, u32[]{:S(2)}) %all-to-all-start.10) | async-done | bytes 16777248 | tf_op jit(solution)/shard_map/all_to_all | solution.py:129
  259.6 20.6 %pad.51 = bf16[11136,1024]{1,0:T(8,128)(2,1)} pad(bf16[8192,1024]{1,0:T(8,128)(2,1)} %bitcast.32, bf16[]{:T(256)} %constant.42.clone.1), padding=0_2944x0_0 | pad | bytes 39583744 | tf_op jit(solution)/shard_map/jit(_pad)/pad | solution.py:21
  283.7 33.7 %while.17 = (s32[]{:T(128)}, bf16[11136,1024]{1,0:T(8,128)(2,1)}, s32[4,2]{0,1:T(2,128)S(1)}, bf16[4,2944,1024]{2,1,0:T(8,128)(2,1)}) while((s32[]{:T(128)}, bf16[11136,1024]{1,0:T(8,128)(2,1)}, s32[4,2]{0,1:T(2,128)S(1)}, bf16[4,2944,1024]{2,1,0:T(8,128)(2,1)}) %tuple.155), condition=%wide.while_cond.5.clone, body=%wide.while_body.5.sunk.clone | while | flops 2 | bytes 12059229 | solution.py:25
  284.3 7.8 %bitcast_dynamic-update-slice_fusion.19 = bf16[4,2944,1024]{2,1,0:T(8,128)(2,1)} fusion(bf16[4,2944,1024]{2,1,0:T(8,128)(2,1)} %get-tuple-element.387, s32[]{:T(128)S(6)} %copy.107, bf16[11136,1024]{1,0:T(8,128)(2,1)} %get-tuple-element.389, s32[]{:T(128)} %bitcast.307), kind=kLoop, calls=%fused_computation.11.clone.1.clone | loop fusion | bytes 12059140 | tf_op jit(solution)/shard_map/vmap()/gather
  292.7 7.8 %bitcast_dynamic-update-slice_fusion.19 = bf16[4,2944,1024]{2,1,0:T(8,128)(2,1)} fusion(bf16[4,2944,1024]{2,1,0:T(8,128)(2,1)} %get-tuple-element.387, s32[]{:T(128)S(6)} %copy.107, bf16[11136,1024]{1,0:T(8,128)(2,1)} %get-tuple-element.389, s32[]{:T(128)} %bitcast.307), kind=kLoop, calls=%fused_computation.11.clone.1.clone | loop fusion | bytes 12059140 | tf_op jit(solution)/shard_map/vmap()/gather
  301.2 7.8 %bitcast_dynamic-update-slice_fusion.19 = bf16[4,2944,1024]{2,1,0:T(8,128)(2,1)} fusion(bf16[4,2944,1024]{2,1,0:T(8,128)(2,1)} %get-tuple-element.387, s32[]{:T(128)S(6)} %copy.107, bf16[11136,1024]{1,0:T(8,128)(2,1)} %get-tuple-element.389, s32[]{:T(128)} %bitcast.307), kind=kLoop, calls=%fused_computation.11.clone.1.clone | loop fusion | bytes 12059140 | tf_op jit(solution)/shard_map/vmap()/gather
  309.6 7.8 %bitcast_dynamic-update-slice_fusion.19 = bf16[4,2944,1024]{2,1,0:T(8,128)(2,1)} fusion(bf16[4,2944,1024]{2,1,0:T(8,128)(2,1)} %get-tuple-element.387, s32[]{:T(128)S(6)} %copy.107, bf16[11136,1024]{1,0:T(8,128)(2,1)} %get-tuple-element.389, s32[]{:T(128)} %bitcast.307), kind=kLoop, calls=%fused_computation.11.clone.1.clone | loop fusion | bytes 12059140 | tf_op jit(solution)/shard_map/vmap()/gather
  321.0 21.3 %broadcast_select_fusion = bf16[4,2944,1024]{2,1,0:T(8,128)(2,1)} fusion(bf16[4,2944,1024]{2,1,0:T(8,128)(2,1)} %get-tuple-element.51, pred[4,2944]{1,0:T(4,128)(4,1)S(1)} %iota_compare_fusion), kind=kLoop, calls=%fused_computation.13 | loop fusion | flops 12058624 | bytes 48246272 | tf_op jit(solution)/shard_map/vmap(jit(_where))/select_n | solution.py:26
  342.3 8.4 %all-to-all-start.11 = ((bf16[4,2944,1024]{2,1,0:T(8,128)(2,1)}), bf16[4,2944,1024]{2,1,0:T(8,128)(2,1)}, u32[]{:S(2)}, u32[]{:S(2)}) async-start(bf16[4,2944,1024]{2,1,0:T(8,128)(2,1)} %broadcast_select_fusion), calls=%async_computation.11 | async-start | bytes 48234496 | tf_op jit(solution)/shard_map/all_to_all | solution.py:130
  360.8 250.8 %all-to-all-done.11 = bf16[4,2944,1024]{2,1,0:T(8,128)(2,1)} async-done(((bf16[4,2944,1024]{2,1,0:T(8,128)(2,1)}), bf16[4,2944,1024]{2,1,0:T(8,128)(2,1)}, u32[]{:S(2)}, u32[]{:S(2)}) %all-to-all-start.11) | async-done | bytes 24117280 | tf_op jit(solution)/shard_map/all_to_all | solution.py:130
  611.6 4.8 all-to-all-start.9
  623.6 20.1 %copy.90 = bf16[4,368,8,1024]{3,2,0,1:T(8,128)(2,1)} copy(bf16[4,368,8,1024]{3,2,1,0:T(8,128)(2,1)} %bitcast.100) | data formatting | bytes 48234496 | tf_op jit(solution)/shard_map/all_to_all | solution.py:130
  643.7 9.7 %fusion.65 = f32[8,4096]{1,0:T(8,128)S(1)} fusion(bf16[2944,4096]{1,0:T(8,128)(2,1)} %bitcast.308, f32[2944,8]{0,1:T(8,128)S(1)} %get-tuple-element.83, f32[2944,8]{0,1:T(8,128)S(1)} %copy-done.13, bf16[2944,4,8]{0,2,1:T(8,128)(2,1)} %bitcast.29, f32[2944]{0:T(1024)S(1)} %pad_dynamic-slice_fusion.3, f32[2944]{0:T(1024)S(1)} %pad_dynamic-slice_fusion.2), kind=kOutput, calls=%fused_computation.154 | convolution fusion | flops 193267712 | bytes 24507392 | tf_op jit(solution)/shard_map/dot_general | solution.py:90
  653.4 5.0 copy-done
  670.5 15.7 %all-reduce.14 = (bf16[8,4096]{1,0:T(8,128)(2,1)S(1)}, bf16[8,4096]{1,0:T(8,128)(2,1)S(1)}, bf16[8,4096]{1,0:T(8,128)(2,1)S(1)}, bf16[8,4096]{1,0:T(8,128)(2,1)S(1)}) all-reduce(f32[8,4096]{1,0:T(8,128)S(1)} %fusion.65, f32[8,4096]{1,0:T(8,128)S(1)} %fusion.67, ...), channel_id=1, replica_groups=mesh['groups'=2,'tp'=4,'dp'=4] {'tp'}, use_global_device_ids=true, to_apply=%region_14.15 | all-reduce | flops 131072 | bytes 786432 | tf_op jit(solution)/shard_map/psum | solution.py:93
  (205 shorter events, 102.8 us)
Async XLA Ops:
  0.6 7.9 %all-to-all-start.8 = ((bf16[2048,4,8]{0,2,1:T(8,128)(2,1)}), bf16[2048,4,8]{0,2,1:T(8,128)(2,1)S(1)}, u32[]{:S(2)}, u32[]{:S(2)}) async-start(bf16[2048,4,8]{0,2,1:T(8,128)(2,1)} %bitcast.326), calls=%async_computation.8 | async-start | bytes 262144 | tf_op jit(solution)/shard_map/all_to_all | solution.py:152
  8.5 9.8 %all-to-all-start.6 = ((bf16[2048,4,8]{0,2,1:T(8,128)(2,1)}), bf16[2048,4,8]{0,2,1:T(8,128)(2,1)S(1)}, u32[]{:S(2)}, u32[]{:S(2)}) async-start(bf16[2048,4,8]{0,2,1:T(8,128)(2,1)} %bitcast.327), calls=%async_computation.6 | async-start | bytes 262144 | tf_op jit(solution)/shard_map/all_to_all | solution.py:151
  18.3 8.8 %all-to-all-start = ((bf16[2048,4,8]{0,2,1:T(8,128)(2,1)}), bf16[2048,4,8]{0,2,1:T(8,128)(2,1)S(1)}, u32[]{:S(2)}, u32[]{:S(2)}) async-start(bf16[2048,4,8]{0,2,1:T(8,128)(2,1)} %bitcast), calls=%async_computation | async-start | bytes 262144 | tf_op jit(solution)/shard_map/all_to_all | solution.py:153
  27.1 9.9 %all-to-all-start.4 = ((f32[2048,4,8]{0,2,1:T(8,128)}), f32[2048,4,8]{0,2,1:T(8,128)S(1)}, u32[]{:S(2)}, u32[]{:S(2)}) async-start(f32[2048,4,8]{0,2,1:T(8,128)} %bitcast.13), calls=%async_computation.4 | async-start | bytes 524288 | tf_op jit(solution)/shard_map/all_to_all | solution.py:35
  36.9 7.8 %all-to-all-start.7 = ((bf16[4,2944,8]{1,2,0:T(8,128)(2,1)}), bf16[4,2944,8]{1,2,0:T(8,128)(2,1)S(1)}, u32[]{:S(2)}, u32[]{:S(2)}) async-start(bf16[4,2944,8]{1,2,0:T(8,128)(2,1)} %get-tuple-element.168), calls=%async_computation.7 | async-start | bytes 376832 | tf_op jit(solution)/shard_map/all_to_all | solution.py:159
  44.7 18.2 %copy-start.5 = (bf16[4,2944,8]{1,2,0:T(8,128)(2,1)}, bf16[4,2944,8]{1,2,0:T(8,128)(2,1)S(1)}, u32[]{:S(2)}) copy-start(bf16[4,2944,8]{1,2,0:T(8,128)(2,1)S(1)} %all-to-all-done.7) | copy-start | bytes 565252
  44.7 18.2 %all-to-all-start.2 = ((f32[2048,4,32]{0,2,1:T(8,128)}), f32[2048,4,32]{0,2,1:T(8,128)S(1)}, u32[]{:S(2)}, u32[]{:S(2)}) async-start(f32[2048,4,32]{0,2,1:T(8,128)} %bitcast.9), calls=%async_computation.2 | async-start | bytes 2097152 | tf_op jit(solution)/shard_map/all_to_all | solution.py:34
  62.9 189.9 %all-to-all-start.10 = ((bf16[2048,4,1024]{2,0,1:T(8,128)(2,1)}), bf16[2048,4,1024]{2,0,1:T(8,128)(2,1)}, u32[]{:S(2)}, u32[]{:S(2)}) async-start(bf16[2048,4,1024]{2,0,1:T(8,128)(2,1)} %bitcast.314), calls=%async_computation.10 | async-start | bytes 33554432 | tf_op jit(solution)/shard_map/all_to_all | solution.py:129
  252.8 27.4 %all-to-all-start.1 = ((bf16[4,2944,8]{1,2,0:T(8,128)(2,1)}), bf16[4,2944,8]{1,2,0:T(8,128)(2,1)S(1)}, u32[]{:S(2)}, u32[]{:S(2)}) async-start(bf16[4,2944,8]{1,2,0:T(8,128)(2,1)} %get-tuple-element.169), calls=%async_computation.1 | async-start | bytes 376832 | tf_op jit(solution)/shard_map/all_to_all | solution.py:161
  280.2 37.2 %all-to-all-start.5 = ((f32[4,2944,8]{1,2,0:T(8,128)}), f32[4,2944,8]{1,2,0:T(8,128)S(1)}, u32[]{:S(2)}, u32[]{:S(2)}) async-start(f32[4,2944,8]{1,2,0:T(8,128)} %broadcast_select_fusion.2), calls=%async_computation.5 | async-start | bytes 753664 | tf_op jit(solution)/shard_map/all_to_all | solution.py:41
  317.4 24.9 %all-to-all-start.3 = ((f32[4,2944,32]{1,2,0:T(8,128)}), f32[4,2944,32]{1,2,0:T(8,128)S(1)}, u32[]{:S(2)}, u32[]{:S(2)}) async-start(f32[4,2944,32]{1,2,0:T(8,128)} %broadcast_select_fusion.1), calls=%async_computation.3 | async-start | bytes 3014656 | tf_op jit(solution)/shard_map/all_to_all | solution.py:40
  342.3 13.6 %copy-start.17 = (f32[8192]{0:T(1024)S(1)}, f32[8192]{0:T(1024)}, u32[]{:S(2)}) copy-start(f32[8192]{0:T(1024)} %param.27) | copy-start | bytes 98308
  342.3 13.6 %copy-start.20 = (f32[4,8,16]{2,1,0:T(8,128)S(1)}, f32[4,8,16]{2,1,0:T(8,128)}, u32[]{:S(2)}) copy-start(f32[4,8,16]{2,1,0:T(8,128)} %param.19) | copy-start | bytes 6148
  342.3 14.2 %copy-start.14 = (f32[8192,4]{0,1:T(4,128)S(1)}, f32[8192,4]{0,1:T(4,128)}, u32[]{:S(2)}) copy-start(f32[8192,4]{0,1:T(4,128)} %param.24) | copy-start | bytes 393220
  342.3 14.3 %copy-start.9 = (f32[8192,16]{0,1:T(8,128)S(1)}, f32[8192,16]{0,1:T(8,128)}, u32[]{:S(2)}) copy-start(f32[8192,16]{0,1:T(8,128)} %param.23) | copy-start | bytes 1572868
  342.3 269.3 %all-to-all-start.11 = ((bf16[4,2944,1024]{2,1,0:T(8,128)(2,1)}), bf16[4,2944,1024]{2,1,0:T(8,128)(2,1)}, u32[]{:S(2)}, u32[]{:S(2)}) async-start(bf16[4,2944,1024]{2,1,0:T(8,128)(2,1)} %broadcast_select_fusion), calls=%async_computation.11 | async-start | bytes 48234496 | tf_op jit(solution)/shard_map/all_to_all | solution.py:130
  359.5 256.9 %copy-start.18 = (f32[8,16]{1,0:T(8,128)S(1)}, f32[8,16]{1,0:T(8,128)}, u32[]{:S(2)}) copy-start(f32[8,16]{1,0:T(8,128)} %get-tuple-element.166) | copy-start | bytes 1540
  360.8 259.2 %copy-start.2 = (f32[2944,8]{0,1:T(8,128)}, f32[2944,8]{0,1:T(8,128)S(1)}, u32[]{:S(2)}) copy-start(f32[2944,8]{0,1:T(8,128)S(1)} %get-tuple-element.144) | copy-start | bytes 282628
  360.8 259.2 %copy-start.3 = (f32[2944,8]{0,1:T(8,128)}, f32[2944,8]{0,1:T(8,128)S(1)}, u32[]{:S(2)}) copy-start(f32[2944,8]{0,1:T(8,128)S(1)} %get-tuple-element.145) | copy-start | bytes 282628
  360.8 259.2 %copy-start.4 = (f32[2944,8]{0,1:T(8,128)}, f32[2944,8]{0,1:T(8,128)S(1)}, u32[]{:S(2)}) copy-start(f32[2944,8]{0,1:T(8,128)S(1)} %get-tuple-element.146) | copy-start | bytes 282628
  611.6 32.0 %all-to-all-start.9 = ((bf16[4,2944,8]{1,2,0:T(8,128)(2,1)}), bf16[4,2944,8]{1,2,0:T(8,128)(2,1)}, u32[]{:S(2)}, u32[]{:S(2)}) async-start(bf16[4,2944,8]{1,2,0:T(8,128)(2,1)} %get-tuple-element.167), calls=%async_computation.9 | async-start | bytes 376832 | tf_op jit(solution)/shard_map/all_to_all | solution.py:160
  623.6 20.1 %copy-start.13 = (f32[2944,8]{0,1:T(8,128)S(1)}, f32[2944,8]{0,1:T(8,128)}, u32[]{:S(2)}) copy-start(f32[2944,8]{0,1:T(8,128)} %get-tuple-element.77) | copy-start | bytes 282628
  643.7 14.7 %copy-start = (bf16[4,368,8,1024]{3,2,0,1:T(8,128)(2,1)S(1)}, bf16[4,368,8,1024]{3,2,0,1:T(8,128)(2,1)}, u32[]{:S(2)}) copy-start(bf16[4,368,8,1024]{3,2,0,1:T(8,128)(2,1)} %copy.90) | copy-start | bytes 72351744
  643.7 14.7 %copy-start.12 = (f32[2944,8]{0,1:T(8,128)S(1)}, f32[2944,8]{0,1:T(8,128)}, u32[]{:S(2)}) copy-start(f32[2944,8]{0,1:T(8,128)} %get-tuple-element.76) | copy-start | bytes 282628
  (13 other events, 84.7 us)
where the time goes:
time: 691 us; the launch traced here: 687 us
  waiting for transfers between devices  419 us (61%)
  local copies, waits for them, and re-layouts  135 us (20%)
  starting transfers between devices  55.4 us (8%)
  other arithmetic  37.4 us (5%)
  matrix products  21.8 us (3%)
  blocking collectives  15.7 us (2%)
    all_to_all x1, waiting for transfers between devices, per_device(): lax.all_to_all(pack_rows(spread_w, accelerator_first_lane, accelerator_to...  251 us
    all_to_all x1, waiting for transfers between devices, per_device(): lax.all_to_all(emission_matrix, 'tp', split_axis=1, concat_axis=0, tiled=...  163 us
    gather x84, local copies, waits for them, and re-layouts  67.1 us
    select_n x4, other arithmetic, one_owner(): jnp.where((places < count * BLOCK)[:, None], rows, jnp.zeros_like(rows))  25.6 us
    dot_general x4, matrix products, decode_steps(): lax.dot_general(gated, weights, (((0,), (0,)), ((), ())), preferred_eleme...  21.8 us
    pad x6, local copies, waits for them, and re-layouts, pack_rows(): padded = jnp.pad(columns, ((0, slot_rows), (0, 0)))  20.8 us
    all_to_all x1, local copies, waits for them, and re-layouts, per_device(): lax.all_to_all(pack_rows(spread_w, accelerator_first_lane, accelerator_to...  20.1 us
    psum x1, blocking collectives, decode_steps(): results.append(lax.psum(partial_out, 'tp').astype(jnp.bfloat16))  15.7 us
  transfers between devices with their start and end apart: 12, of which 4 were waited for; matrix products, arithmetic and copies ran while one was open for 24% of the time, Pallas kernels for 0%

commit v1 on v0

v1 whole, which is shorter than its diff:
```python
import jax
import jax.numpy as jnp
from jax import lax
from jax.experimental import pallas as pl
from jax.experimental.pallas import tpu as pltpu
from jax.sharding import PartitionSpec as P

BLOCK = 128
UNIT = 16
BF = jnp.bfloat16
F32 = jnp.float32
AXES = ("groups", "tp", "dp")


def owner_ranges(remaining_ranks, holder_segment_tallies, holder_ranks):
    starts = jnp.cumsum(holder_segment_tallies) - holder_segment_tallies
    roster = jnp.arange(holder_ranks, dtype=jnp.int32)
    match = (remaining_ranks[None, :] == roster[:, None]).astype(jnp.int32)
    first = jnp.sum(match * starts[None, :], axis=1)
    total = jnp.sum(match * holder_segment_tallies[None, :], axis=1)
    return first, total


def pack_rows(columns, first, total, slot_rows):
    padded = jnp.pad(columns, ((0, slot_rows), (0, 0)))
    places = jnp.arange(slot_rows, dtype=jnp.int32)

    def one_owner(start, count):
        rows = lax.dynamic_slice_in_dim(padded, start * BLOCK, slot_rows, 0)
        return jnp.where((places < count * BLOCK)[:, None], rows, jnp.zeros_like(rows))

    packed = jax.vmap(one_owner)(first, total)
    return packed.reshape(-1, columns.shape[1])


def relocate_everywhere(rows, first, total, slot_rows):
    spread = lax.all_to_all(rows, "tp", split_axis=1, concat_axis=0, tiled=True)
    packed = pack_rows(spread, first, total, slot_rows)
    return lax.all_to_all(packed, "tp", split_axis=0, concat_axis=1, tiled=True)


def decode_plain(x, z, dt, enter, leave, ssm, conv, logs, taps, offs, inc, res, weights):
    steps, seqs, channels = x.shape
    h = ssm.reshape(channels, seqs, -1)
    window = conv.reshape(channels, seqs, 4)
    decay = -jnp.exp(logs)
    gated = []
    for step in range(steps):
        now = x[step].astype(F32).T
        window = jnp.concatenate([window[:, :, 1:], now[:, :, None]], axis=2)
        inner = jax.nn.silu(jnp.sum(window * taps[:, None, :], axis=2) + offs[:, None])
        delta = jax.nn.softplus(dt[step].astype(F32).T + inc[:, None])
        h = (
            jnp.exp(delta[:, :, None] * decay[:, None, :]) * h
            + (delta * inner)[:, :, None] * enter[step][None, :, :]
        )
        y = jnp.sum(h * leave[step][None, :, :], axis=2) + res[:, None] * inner
        gated.append((y * jax.nn.silu(z[step].astype(F32).T)).astype(BF))
    gated = jnp.concatenate(gated, axis=1)
    partial = lax.dot_general(
        gated, weights, (((0,), (0,)), ((), ())), preferred_element_type=F32
    )
    return partial, h.reshape(channels, -1), window.reshape(channels, -1)


def general(x, z, dt, enter, leave, w, ssm, conv, logs, taps, offs, inc, res, ranks, tallies):
    holders = lax.axis_size("tp")
    mine = lax.axis_index("tp")
    width, old = logs.shape[0], w.shape[0]
    slot_rows = (width // BLOCK // (holders * 3 // 4) + 2) * BLOCK
    first, total = owner_ranges(ranks, tallies, holders)

    def own(a):
        return lax.dynamic_slice_in_dim(a, mine * old, old, 0)

    moved_w = relocate_everywhere(w, first, total, slot_rows)
    partial, ssm, conv = decode_plain(
        x, z, dt, enter, leave, ssm, conv, own(logs), own(taps), own(offs), own(inc), own(res), w
    )
    decoded = lax.psum(partial, "tp").astype(BF).reshape(x.shape[0], x.shape[1], -1)
    return (
        decoded,
        moved_w,
        relocate_everywhere(ssm, first, total, slot_rows),
        relocate_everywhere(conv, first, total, slot_rows),
    )


CHUNK = 256


def decode_kernel(
    sc, x, z, dt, enter, leave, h0, hist, logs, taps, offs, inc, res, w,
    out_w, partial, states, ys, blank, own_sem, blank_sem,
):
    i = pl.program_id(0)
    steps, seqs, chunk = x.shape
    latents = logs.shape[0]
    per = chunk // BLOCK
    slots = out_w.shape[0] // BLOCK
    own_src, own_n, own_dst, filled = sc[1], sc[2], sc[3], sc[4]

    def blank_copy(b):
        return pltpu.make_async_copy(blank, out_w.at[pl.ds(b * BLOCK, BLOCK)], blank_sem.at[b])

    @pl.when(i == 0)
    def _():
        blank[...] = jnp.zeros_like(blank)
        partial[...] = jnp.zeros_like(partial)
        for b in range(slots):

            @pl.when(b >= filled)
            def _():
                blank_copy(b).start()

    def own_copy(j):
        at = jnp.clip(i * per + j - own_src + own_dst, 0, slots - 1)
        return pltpu.make_async_copy(
            w.at[pl.ds(j * BLOCK, BLOCK)],
            out_w.at[pl.ds(pl.multiple_of(at * BLOCK, BLOCK), BLOCK)],
            own_sem.at[j],
        )

    def is_own(j):
        b = i * per + j
        return (b >= own_src) & (b < own_src + own_n)

    for j in range(per):

        @pl.when(is_own(j))
        def _():
            own_copy(j).start()

    decay = -jnp.exp(logs[...])
    xs = [x[t].astype(F32) for t in range(steps)]
    window = [hist[k] for k in range(1, 4)] + xs
    tap = [taps[k : k + 1, :] for k in range(4)]
    inners, deltas, feeds = [], [], []
    for t in range(steps):
        mixed = offs[...] + sum(window[t + k] * tap[k] for k in range(4))
        inner = mixed / (1.0 + jnp.exp(-mixed))
        v = dt[t].astype(F32) + inc[...]
        delta = jnp.maximum(v, 0.0) + jnp.log1p(jnp.exp(-jnp.abs(v)))
        inners.append(inner)
        deltas.append(delta)
        feeds.append(delta * inner)
    turned = h0[...].T
    for s in range(seqs):
        h = turned[s * latents : (s + 1) * latents]
        for t in range(steps):
            c = t * seqs + s
            h = (
                jnp.exp(deltas[t][s : s + 1] * decay) * h
                + feeds[t][s : s + 1] * enter[:, c : c + 1]
            )
            ys[c : c + 1, :] = jnp.sum(h * leave[:, c : c + 1], axis=0, keepdims=True)
        states[s * latents : (s + 1) * latents, :] = h.astype(BF)
    states[seqs * latents :, :] = jnp.concatenate(xs, axis=0).astype(BF)
    gated = []
    for t in range(steps):
        y = ys[t * seqs : (t + 1) * seqs, :] + res[...] * inners[t]
        g = z[t].astype(F32)
        gated.append(y * (g / (1.0 + jnp.exp(-g))))
    gated = jnp.concatenate(gated, axis=0).astype(BF)
    partial[...] += jnp.dot(gated, w[...], preferred_element_type=F32)

    for j in range(per):

        @pl.when(is_own(j))
        def _():
            own_copy(j).wait()

    @pl.when(i == pl.num_programs(0) - 1)
    def _():
        for b in range(slots):

            @pl.when(b >= filled)
            def _():
                blank_copy(b).wait()


def decode_here(scalars, slots, x, z, dt, enter, leave, w, ssm, conv, logs, taps, offs, inc, res):
    steps, seqs, channels = x.shape
    latents = logs.shape[1]
    features = w.shape[1]
    n = channels // CHUNK
    series = pl.BlockSpec((steps, seqs, CHUNK), lambda i, sc: (0, 0, i))
    small = pl.BlockSpec((latents, steps * seqs), lambda i, sc: (0, 0))

    def lanes(rows):
        return pl.BlockSpec((rows, CHUNK), lambda i, sc: (0, sc[0] * n + i))

    grid_spec = pltpu.PrefetchScalarGridSpec(
        num_scalar_prefetch=1,
        grid=(n,),
        in_specs=[
            series, series, series, small, small,
            pl.BlockSpec((CHUNK, seqs * latents), lambda i, sc: (i, 0)),
            pl.BlockSpec((4, seqs, CHUNK), lambda i, sc: (0, 0, i)),
            lanes(latents), lanes(4), lanes(1), lanes(1), lanes(1),
            pl.BlockSpec((CHUNK, features), lambda i, sc: (i, 0)),
        ],
        out_specs=[
            pl.BlockSpec(memory_space=pl.ANY),
            pl.BlockSpec((steps * seqs, features), lambda i, sc: (0, 0)),
            pl.BlockSpec((seqs * (latents + 4), CHUNK), lambda i, sc: (0, i)),
        ],
        scratch_shapes=[
            pltpu.VMEM((steps * seqs, CHUNK), F32),
            pltpu.VMEM((BLOCK, features), BF),
            pltpu.SemaphoreType.DMA((CHUNK // BLOCK,)),
            pltpu.SemaphoreType.DMA((slots,)),
        ],
    )
    rows = steps * seqs
    return pl.pallas_call(
        decode_kernel,
        grid_spec=grid_spec,
        out_shape=(
            jax.ShapeDtypeStruct((slots * BLOCK, features), BF),
            jax.ShapeDtypeStruct((rows, features), F32),
            jax.ShapeDtypeStruct((seqs * (latents + 4), channels), BF),
        ),
        compiler_params=pltpu.CompilerParams(vmem_limit_bytes=24 << 20),
        cost_estimate=pl.CostEstimate(
            flops=2 * rows * channels * features,
            bytes_accessed=2 * 2 * channels * features,
            transcendentals=rows * channels * latents,
        ),
        name="decode",
    )(
        scalars, x, z, dt,
        enter.transpose(2, 0, 1).reshape(latents, rows),
        leave.transpose(2, 0, 1).reshape(latents, rows),
        ssm, conv.T.reshape(seqs, 4, channels).transpose(1, 0, 2), logs.T, taps.T,
        offs.reshape(1, -1), inc.reshape(1, -1), res.reshape(1, -1), w,
    )


def place_rows(scalars, out_w, pieces, side=None):
    slots = out_w.shape[0] // BLOCK
    n = len(pieces)
    arrays = []
    for piece in pieces:
        if not any(piece[0] is a for a in arrays):
            arrays.append(piece[0])
    which = [next(k for k, a in enumerate(arrays) if a is piece[0]) for piece in pieces]
    shapes = [piece[1:] for piece in pieces]
    side_n = 0 if side is None else side.shape[0] // BLOCK
    operands = arrays + ([] if side is None else [side])

    def kernel(sc, *refs):
        ins, out = refs[: len(operands)], refs[len(operands) + 1]
        sems, side_sems = refs[-2], refs[-1]
        recv, row0, q = sc[5], sc[6], sc[7]
        c_src, c_n, c_dst = sc[8], sc[9], sc[10]

        def copies():
            for k, (first, rows, offset) in enumerate(shapes):
                at = jnp.clip(row0 + offset(q) * UNIT, 0, slots * BLOCK - rows)
                yield pltpu.make_async_copy(
                    ins[which[k]].at[pl.ds(first, rows)],
                    out.at[pl.ds(pl.multiple_of(at, UNIT), rows)],
                    sems.at[k],
                )

        def side_copy(b):
            src = jnp.clip(c_src + b, 0, side_n - 1) * BLOCK
            dst = jnp.clip(c_dst + b, 0, slots - 1) * BLOCK
            return pltpu.make_async_copy(
                ins[-1].at[pl.ds(pl.multiple_of(src, BLOCK), BLOCK)],
                out.at[pl.ds(pl.multiple_of(dst, BLOCK), BLOCK)],
                side_sems.at[b],
            )

        @pl.when(recv == 1)
        def _():
            for copy in copies():
                copy.start()

        for b in range(side_n):

            @pl.when(b < c_n)
            def _():
                side_copy(b).start()

        @pl.when(recv == 1)
        def _():
            for copy in copies():
                copy.wait()

        for b in range(side_n):

            @pl.when(b < c_n)
            def _():
                side_copy(b).wait()

    any_spec = pl.BlockSpec(memory_space=pl.ANY)
    moved = sum(s[1] for s in shapes) * out_w.shape[1] * 4
    return pl.pallas_call(
        kernel,
        grid_spec=pltpu.PrefetchScalarGridSpec(
            num_scalar_prefetch=1,
            grid=(),
            in_specs=[any_spec] * (len(operands) + 1),
            out_specs=any_spec,
            scratch_shapes=[
                pltpu.SemaphoreType.DMA((n,)),
                pltpu.SemaphoreType.DMA((max(side_n, 1),)),
            ],
        ),
        out_shape=jax.ShapeDtypeStruct(out_w.shape, out_w.dtype),
        input_output_aliases={len(operands) + 1: 0},
        cost_estimate=pl.CostEstimate(flops=0, bytes_accessed=moved, transcendentals=0),
        name="place_rows",
    )(scalars, *operands, out_w)


def place_states(scalars, slots, own, side, across, latent_rows):
    rows = own.shape[0]
    seqs = (rows - latent_rows) // 4

    def kernel(sc, own_ref, side_ref, across_ref, ssm, conv, turned):
        own_src, own_n, own_dst, filled = sc[1], sc[2], sc[3], sc[4]
        recv, recv_dst = sc[5], sc[6] // BLOCK
        c_src, c_n, c_dst = sc[8], sc[9], sc[10]

        def put(b, ref, at):
            block = ref[:, pl.ds(pl.multiple_of(at * BLOCK, BLOCK), BLOCK)].astype(F32)
            ssm[b * BLOCK : (b + 1) * BLOCK, :] = block[:latent_rows].T
            for k in range(4):
                at = latent_rows + k * seqs
                turned[pl.ds(k, seqs, stride=4), :] = block[at : at + seqs]
            conv[:, b * BLOCK : (b + 1) * BLOCK] = turned[...]

        across_n = across_ref.shape[1] // BLOCK
        for b in range(slots):
            in_own = (b >= own_dst) & (b < own_dst + own_n)
            in_side = (b >= c_dst) & (b < c_dst + c_n)
            in_across = (recv == 1) & (b >= recv_dst) & (b < recv_dst + across_n)

            @pl.when(in_own)
            def _():
                put(b, own_ref, b - own_dst + own_src)

            @pl.when(in_side)
            def _():
                put(b, side_ref, b - c_dst + c_src)

            @pl.when(in_across)
            def _():
                put(b, across_ref, b - recv_dst)

            @pl.when(b >= filled)
            def _():
                ssm[b * BLOCK : (b + 1) * BLOCK, :] = jnp.zeros((BLOCK, latent_rows), F32)
                conv[:, b * BLOCK : (b + 1) * BLOCK] = jnp.zeros((rows - latent_rows, BLOCK), F32)

    vmem = pl.BlockSpec(memory_space=pltpu.VMEM)
    return pl.pallas_call(
        kernel,
        grid_spec=pltpu.PrefetchScalarGridSpec(
            num_scalar_prefetch=1,
            grid=(),
            in_specs=[vmem] * 3,
            out_specs=[vmem] * 2,
            scratch_shapes=[pltpu.VMEM((rows - latent_rows, BLOCK), F32)],
        ),
        out_shape=(
            jax.ShapeDtypeStruct((slots * BLOCK, latent_rows), F32),
            jax.ShapeDtypeStruct((rows - latent_rows, slots * BLOCK), F32),
        ),
        compiler_params=pltpu.CompilerParams(vmem_limit_bytes=24 << 20),
        name="place_states",
    )(scalars, own, side, across)


def neighbours(x, z, dt, enter, leave, w, ssm, conv, logs, taps, offs, inc, res, ranks, tallies):
    groups, depth = lax.axis_size("groups"), lax.axis_size("dp")
    g, t, d = (lax.axis_index(a) for a in AXES)
    old_blocks = w.shape[0] // BLOCK
    cap = (logs.shape[0] // BLOCK) // 3 + 2
    most = cap - old_blocks
    half = 2 * old_blocks

    def place(a, b, c):
        return (a * 4 + b) * depth + c

    every = [(a, c) for a in range(groups) for c in range(depth)]
    across = [(place(a, u, c), place(a, 3 - u, c)) for a, c in every for u in (1, 2)]
    along_x = [(place(a, u, c), place(1 - a, u, c)) for a, c in every for u in (1, 2)]
    along_z = [(place(a, u, c), place(a, u, c ^ 1)) for a, c in every for u in (1, 2)]
    inside = [(place(a, u, c), place(a, v, c)) for a, c in every for u, v in ((1, 0), (2, 3))]
    cores = [(place(a, u, c), place(a, u ^ 1, c)) for a, c in every for u in range(4)]
    chips = [(place(a, u, c), place(a, u ^ 2, c)) for a, c in every for u in range(4)]

    q = 2 * g + (d & 1)
    middle = ranks[1]
    t0, t1, t2 = tallies[0], tallies[1], tallies[2]
    is_mid = (t == middle).astype(jnp.int32)
    crossing = jnp.where(middle == 2, half - t0, half - t2)

    def by_rank(first, low, high, last):
        return jnp.where(t == 0, first, jnp.where(t == 3, last, jnp.where(t == 1, low, high)))

    own_src = by_rank(0, t0 - old_blocks, 0, 0)
    own_n = by_rank(old_blocks, is_mid * (half - t0), is_mid * (half - t2), old_blocks)
    own_dst = by_rank(0, 0, crossing, t2 - old_blocks)
    filled = by_rank(t0, is_mid * t1, is_mid * t1, t2)
    row0 = by_rank(0, (half - t0) * BLOCK, 0, 0)
    c_src = by_rank(0, 0, 0, most - (t2 - old_blocks))
    c_n = by_rank(t0 - old_blocks, 0, 0, t2 - old_blocks)
    c_dst = by_rank(old_blocks, 0, 0, 0)
    scalars = jnp.stack(
        [t, own_src, own_n, own_dst, filled, is_mid, row0, q, c_src, c_n, c_dst]
    ).astype(jnp.int32)

    def permute(a, pairs):
        return lax.ppermute(a, AXES, pairs)

    def body(v, args):
        scalars, x, z, dt, enter, leave, w, ssm, conv, logs, taps, offs, inc, res = args
        part = v
        relay = v // 2
        base = jnp.where(t == 1, (old_blocks - v) * BLOCK, 0)

        def cut(unit, units):
            return lax.dynamic_slice_in_dim(w, base + unit * UNIT, units * UNIT, 0)

        far = 3 - q
        near_x, near_z = q ^ 2, q ^ 1
        y1 = permute(cut(2 * part * q, part), across)
        side_w = lax.dynamic_slice_in_dim(
            w, jnp.where(t == 1, 0, (old_blocks - most) * BLOCK), most * BLOCK, 0
        )
        side = permute(side_w, inside)
        out_w, partial, states = decode_here(
            scalars, cap, x, z, dt, enter, leave, w, ssm, conv, logs, taps, offs, inc, res
        )
        y2 = permute(cut(2 * part * q + part, part), across)
        x1, z1 = permute(y1, along_x), permute(y1, along_z)
        y3 = permute(cut(2 * part * far + 2 * relay, 2 * part - 2 * relay), across)
        x2 = permute(jnp.concatenate([y2, z1[: relay * UNIT]]), along_x)
        z2 = permute(jnp.concatenate([y2, x1[relay * UNIT : 2 * relay * UNIT]]), along_z)

        features = partial.shape[1]
        core = (t & 1) * (features // 2)
        mine = lax.dynamic_slice_in_dim(partial, core, features // 2, 1)
        theirs = lax.dynamic_slice_in_dim(partial, features // 2 - core, features // 2, 1)
        chip_sum = (mine + permute(theirs, cores)).astype(BF)
        total = (chip_sum.astype(F32) + permute(chip_sum, chips).astype(F32)).astype(BF)
        other = permute(total, cores)
        low = (t & 1) == 0
        decoded = jnp.concatenate(
            [jnp.where(low, total, other), jnp.where(low, other, total)], axis=1
        )

        rows = states.shape[0]
        side_s = permute(
            lax.dynamic_slice_in_dim(
                states, jnp.where(t == 1, 0, (old_blocks - most) * BLOCK), most * BLOCK, 1
            ),
            inside,
        )
        across_s = permute(
            lax.dynamic_slice_in_dim(states, base, v * BLOCK, 1), across
        )
        n = part * UNIT
        out_w = place_rows(
            scalars,
            out_w,
            [
                (y1, 0, n, lambda q: 2 * part * q),
                (x1, 0, n, lambda q: 2 * part * (q ^ 2)),
                (z1, 0, n, lambda q: 2 * part * (q ^ 1)),
            ],
            side,
        )
        m = relay * UNIT
        out_w = place_rows(
            scalars,
            out_w,
            [
                (y2, 0, n, lambda q: 2 * part * q + part),
                (x2, 0, n, lambda q: 2 * part * (q ^ 2) + part),
                (z2, 0, n, lambda q: 2 * part * (q ^ 1) + part),
                (x2, n, m, lambda q: 2 * part * (3 - q)),
                (z2, n, m, lambda q: 2 * part * (3 - q) + relay),
                (y3, 0, 2 * n - 2 * m, lambda q: 2 * part * (3 - q) + 2 * relay),
            ],
        )
        latent_rows = ssm.shape[1]
        new_ssm, new_conv = place_states(scalars, cap, states, side_s, across_s, latent_rows)
        return decoded, out_w, new_ssm, new_conv

    args = (scalars, x, z, dt, enter, leave, w, ssm, conv, logs, taps, offs, inc, res)
    fewest = half - cap
    branches = [lambda args, v=v: body(v, args) for v in range(fewest, old_blocks - 1)]
    decoded, out_w, new_ssm, new_conv = lax.switch(crossing - fewest, branches, args)
    return decoded.reshape(x.shape[0], x.shape[1], -1), out_w, new_ssm, new_conv.T


def solution(mesh):
    placed = (
        P(None, ("groups", "dp"), "tp"),
        P(None, ("groups", "dp"), "tp"),
        P(None, ("groups", "dp"), "tp"),
        P(None, ("groups", "dp"), None),
        P(None, ("groups", "dp"), None),
        P("tp", None),
        P("tp", ("groups", "dp")),
        P("tp", ("groups", "dp")),
    ) + (P(),) * 7
    square = mesh.shape["tp"] == 4 and mesh.shape["groups"] == 2 and mesh.shape["dp"] % 2 == 0
    return jax.shard_map(
        neighbours if square else general,
        mesh=mesh,
        in_specs=placed,
        out_specs=(
            P(None, ("groups", "dp"), None),
            P(("groups", "tp"), None),
            P("tp", ("groups", "dp")),
            P("tp", ("groups", "dp")),
        ),
        check_vma=False,
    )
```

time: 691 us -> 425 us (0.62)
  waiting for transfers between devices: 419 us -> 26.6 us
  Pallas kernels: 0 us -> 311 us
  local copies, waits for them, and re-layouts: 135 us -> 19.1 us
  other arithmetic: 37.4 us -> 4.26 us
  starting transfers between devices: 55.4 us -> 32.3 us
  matrix products: 21.8 us -> 0 us
  loops' own time: 0.41 us -> 17.1 us
  blocking collectives: 15.7 us -> 0 us
    all_to_all x12 -> x0, waiting for transfers between devices: 419 us -> none  [the longest x1 251 us: per_device(): lax.all_to_all(pack_rows(spread_w, accelerator_first_lane, accelerator_to...]
    pallas_call x0 -> x4, Pallas kernels: none -> 311 us  [the longest x2 289 us: place_rows(): pl.pallas_call(kernel, grid_spec=pltpu.PrefetchScalarGridSpec(num_scalar_...]
    gather x84 -> x0, local copies, waits for them, and re-layouts: 67.1 us -> none
    all_to_all x12 -> x0, starting transfers between devices: 55.4 us -> none  [the longest x1 8.4 us: per_device(): lax.all_to_all(pack_rows(spread_w, accelerator_first_lane, accelerator_to...]
    all_to_all x3 -> x0, local copies, waits for them, and re-layouts: 34 us -> none  [the longest x1 20.1 us: per_device(): lax.all_to_all(pack_rows(spread_w, accelerator_first_lane, accelerator_to...]
    ppermute x0 -> x13, starting transfers between devices: none -> 32.3 us  [permute(): return lax.ppermute(a, AXES, pairs)]
    select_n x7 -> x1, other arithmetic: 28.3 us -> 0.03 us  [body(): jnp.where(low, total, other)]
    ppermute x0 -> x13, waiting for transfers between devices: none -> 26.6 us  [permute(): return lax.ppermute(a, AXES, pairs)]
  transfers between devices with their start and end apart: 12 -> 13, of which waited for: 4 -> 3; matrix products, arithmetic and copies ran while one was open for 24% -> 3% of each run, Pallas kernels for 0% -> 31%
where the time goes in v1:
time: 425 us; the launch traced here: 418 us
  Pallas kernels  311 us (73%)
  starting transfers between devices  32.3 us (8%)
  waiting for transfers between devices  26.6 us (6%)
  local copies, waits for them, and re-layouts  19.1 us (4%)
  loops' own time  17.1 us (4%)
  between operations  7.6 us (2%)
  other arithmetic  4.26 us (1%)
    pallas_call x2, Pallas kernels, place_rows(): pl.pallas_call(kernel, grid_spec=pltpu.PrefetchScalarGridSpec(num_scalar_...  289 us
    ppermute x13, starting transfers between devices, permute(): return lax.ppermute(a, AXES, pairs)  32.3 us
    ppermute x13, waiting for transfers between devices, permute(): return lax.ppermute(a, AXES, pairs)  26.6 us
    pallas_call x1, Pallas kernels, decode_here(): pl.pallas_call(decode_kernel, grid_spec=grid_spec, out_shape=(jax.ShapeDt...  17.3 us
    another operation x1, loops' own time, neighbours(): lax.switch(crossing - fewest, branches, args)  17.1 us
  transfers between devices with their start and end apart: 13, of which 3 were waited for; matrix products, arithmetic and copies ran while one was open for 3% of the time, Pallas kernels for 31%

profile of v1, /device:TPU:1, one launch (start us, length us, event | category | flops | bytes accessed | tf_op | source)
XLA Modules:
  0.0 417.9 jit_solution(15587198971714051900)
XLA Ops:
  0.6 1.2 slice.48
  2.5 1.4 fusion
  9.8 407.0 %conditional.1 = (bf16[2944,4096]{1,0:T(8,128)(2,1)}, f32[2944,128]{1,0:T(8,128)}, f32[32,2944]{1,0:T(8,128)}, bf16[4,8,4096]{2,1,0:T(8,128)(2,1)}) conditional(s32[]{:T(128)} %clamp.3, (s32[]{:T(128)}, s32[]{:T(128)}, bf16[2048,4096]{1,0:T(8,128)(2,1)}, f32[4,8,16]{2,1,0:T(8,128)}, f32[4,8,16]{2,1,0:T(8,128)}, ...), branch_computations={%region_0.1_spmd, %region_1.2_spmd, %region_2.3_spmd, %region_3.4_... | conditional | flops 547553280 | bytes 239281712 | solution.py:499
  9.8 7.1 %constant_dynamic-slice_fusion.3 = bf16[896,4096]{1,0:T(8,128)(2,1)} fusion(bf16[2048,4096]{1,0:T(8,128)(2,1)} %get-tuple-element.194.w, s32[]{:T(128)S(6)} %select_n.207), kind=kLoop, calls=%fused_computation.11 | loop fusion | bytes 14680068 | tf_op jit(solution)/shard_map/cond/branch_0_fun/dynamic_slice | solution.py:433
  16.8 4.9 %collective-permute-start.7 = (bf16[896,4096]{1,0:T(8,128)(2,1)}, bf16[896,4096]{1,0:T(8,128)(2,1)}, u32[]{:S(2)}, u32[]{:S(2)}) collective-permute-start(bf16[896,4096]{1,0:T(8,128)(2,1)} %constant_dynamic-slice_fusion.3), channel_id=1, source_target_pairs={{4,0},{8,12},{5,1},{9,13},{6,2},{10,14},{7,3},{11,15},{20,16},{24,... | collective-permute-start | bytes 22020104 | tf_op jit(solution)/shard_map/cond/branch_0_fun/ppermute | solution.py:419
  21.8 3.5 constant_dynamic-slice_fusion.5
  25.2 4.3 %collective-permute-start.1 = (bf16[144,4096]{1,0:T(8,128)(2,1)}, bf16[144,4096]{1,0:T(8,128)(2,1)}, u32[]{:S(2)}, u32[]{:S(2)}) collective-permute-start(bf16[144,4096]{1,0:T(8,128)(2,1)} %get-tuple-element.427), channel_id=1, source_target_pairs={{4,8},{8,4},{5,9},{9,5},{6,10},{10,6},{7,11},{11,7},{20,24},{24,20... | collective-permute-start | bytes 3538952 | tf_op jit(solution)/shard_map/cond/branch_0_fun/ppermute | solution.py:419
  29.6 1.9 collective-permute-start
  31.9 17.3 %decode.6 = (bf16[2944,4096]{1,0:T(8,128)(2,1)}, f32[32,4096]{1,0:T(8,128)S(1)}, bf16[160,2048]{1,0:T(8,128)(2,1)S(1)}) custom-call(s32[11]{0:T(128)} %get-tuple-element.193.sc, bf16[4,8,2048]{2,1,0:T(8,128)(2,1)S(1)} %copy-done.25, bf16[4,8,2048]{2,1,0:T(8,128)(2,1)S(1)} %copy-done.31, bf16[4,8,2048]{2,1,0:T(8,128)(2,1)S(1)} %copy-done.37, ...), custom_call_target="tpu_custom_call" | custom-call | flops 536870912 | bytes 33554432 | tf_op jit(solution)/shard_map/cond/branch_0_fun/decode/pallas_call | solution.py:216
  49.3 4.0 collective-permute-start.2
  53.3 3.1 collective-permute-start.4
  56.5 2.5 constant_dynamic-slice_fusion.4
  59.1 2.4 collective-permute-start.8
  61.5 5.5 %collective-permute-done.2.refs_2_ = bf16[144,4096]{1,0:T(8,128)(2,1)S(1)} collective-permute-done((bf16[144,4096]{1,0:T(8,128)(2,1)}, bf16[144,4096]{1,0:T(8,128)(2,1)S(1)}, u32[]{:S(2)}, u32[]{:S(2)}) %collective-permute-start.2) | collective-permute-done | bytes 1179680 | tf_op jit(solution)/shard_map/cond/branch_0_fun/ppermute | solution.py:419
  67.1 3.6 collective-permute-done.4.refs_1_
  71.8 3.4 pad_maximum_fusion
  75.3 3.1 collective-permute-start.3
  78.4 1.9 collective-permute-start.5
  80.4 4.7 %collective-permute-start.6 = (bf16[160,4096]{1,0:T(8,128)(2,1)}, bf16[160,4096]{1,0:T(8,128)(2,1)}, u32[]{:S(2)}, u32[]{:S(2)}) collective-permute-start(bf16[160,4096]{1,0:T(8,128)(2,1)} %constant_dynamic-slice_fusion.4), channel_id=1, source_target_pairs={{4,8},{8,4},{5,9},{9,5},{6,10},{10,6},{7,11},{11,7},{20,24},{24,20... | collective-permute-start | bytes 3932168 | tf_op jit(solution)/shard_map/cond/branch_0_fun/ppermute | solution.py:419
  85.1 1.9 collective-permute-start.9
  87.0 17.5 %collective-permute-done.9.across_ref = bf16[160,1152]{1,0:T(8,128)(2,1)S(1)} collective-permute-done((bf16[160,1152]{1,0:T(8,128)(2,1)S(1)}, bf16[160,1152]{1,0:T(8,128)(2,1)S(1)}, u32[]{:S(2)}, u32[]{:S(2)}) %collective-permute-start.9) | collective-permute-done | bytes 368672 | tf_op jit(solution)/shard_map/cond/branch_0_fun/ppermute | solution.py:419
  104.5 4.3 %place_states.6 = (f32[2944,128]{1,0:T(8,128)}, f32[32,2944]{1,0:T(8,128)}) custom-call(s32[11]{0:T(128)S(1)} %copy-done.60, bf16[160,2048]{1,0:T(8,128)(2,1)S(1)} %get-tuple-element.210.own_ref, bf16[160,896]{1,0:T(8,128)(2,1)S(1)} %collective-permute-done.8.side_ref, bf16[160,1152]{1,0:T(8,128)(2,1)S(1)} %collective-permute-done.9.across_ref), custom_call_target="tpu_custom_call" | custom-call | tf_op jit(solution)/shard_map/cond/branch_0_fun/place_states/pallas_call | solution.py:360
  109.5 108.9 %place_rows.12.refs_4_ = bf16[2944,4096]{1,0:T(8,128)(2,1)} custom-call(s32[11]{0:T(128)S(1)} %copy-done.60, bf16[144,4096]{1,0:T(8,128)(2,1)} %collective-permute-done.1.refs_0_, bf16[144,4096]{1,0:T(8,128)(2,1)} %collective-permute-done.4.refs_1_, bf16[144,4096]{1,0:T(8,128)(2,1)} %copy-done.45, ...), custom_call_target="tpu_custom_call", output_to_operand_aliasing={{}: (5, {})} | custom-call | bytes 7077888 | tf_op jit(solution)/shard_map/cond/branch_0_fun/place_rows/pallas_call | solution.py:300
  219.7 180.4 %place_rows.13 = bf16[2944,4096]{1,0:T(8,128)(2,1)} custom-call(s32[11]{0:T(128)S(1)} %copy-done.60, bf16[144,4096]{1,0:T(8,128)(2,1)} %collective-permute-done.refs_0_, bf16[208,4096]{1,0:T(8,128)(2,1)} %copy-done.47, bf16[208,4096]{1,0:T(8,128)(2,1)} %collective-permute-done.5.refs_2_, ...), custom_call_target="tpu_custom_call", output_to_operand_aliasing={{}: (5, {})} | custom-call | bytes 11796480 | tf_op jit(solution)/shard_map/cond/branch_0_fun/place_rows/pallas_call | solution.py:300
  (51 shorter events, 4.4 us)
Async XLA Ops:
  16.8 92.7 %collective-permute-start.7 = (bf16[896,4096]{1,0:T(8,128)(2,1)}, bf16[896,4096]{1,0:T(8,128)(2,1)}, u32[]{:S(2)}, u32[]{:S(2)}) collective-permute-start(bf16[896,4096]{1,0:T(8,128)(2,1)} %constant_dynamic-slice_fusion.3), channel_id=1, source_target_pairs={{4,0},{8,12},{5,1},{9,13},{6,2},{10,14},{7,3},{11,15},{20,16},{24,... | collective-permute-start | bytes 22020104 | tf_op jit(solution)/shard_map/cond/branch_0_fun/ppermute | solution.py:419
  21.7 9.8 %copy-start.12 = (f32[2048,32]{0,1:T(8,128)S(1)}, f32[2048,32]{0,1:T(8,128)}, u32[]{:S(2)}) copy-start(f32[2048,32]{0,1:T(8,128)} %get-tuple-element.203) | copy-start | bytes 786436 | tf_op jit(solution)/shard_map/cond
  21.7 10.0 %copy-start.48 = (f32[4,8,16]{2,1,0:T(8,128)S(1)}, f32[4,8,16]{2,1,0:T(8,128)}, u32[]{:S(2)}) copy-start(f32[4,8,16]{2,1,0:T(8,128)} %get-tuple-element.200) | copy-start | bytes 6148 | tf_op jit(solution)/shard_map/cond
  21.7 10.1 %copy-start.54 = (f32[4,8,16]{2,1,0:T(8,128)S(1)}, f32[4,8,16]{2,1,0:T(8,128)}, u32[]{:S(2)}) copy-start(f32[4,8,16]{2,1,0:T(8,128)} %get-tuple-element.201) | copy-start | bytes 6148 | tf_op jit(solution)/shard_map/cond
  21.7 10.2 %copy-start = (f32[2048,128]{1,0:T(8,128)S(1)}, f32[2048,128]{1,0:T(8,128)}, u32[]{:S(2)}) copy-start(f32[2048,128]{1,0:T(8,128)} %get-tuple-element.202.h0) | copy-start | bytes 3145732 | tf_op jit(solution)/shard_map/cond
  21.7 10.2 %copy-start.6 = (f32[8192,16]{0,1:T(8,128)S(1)}, f32[8192,16]{0,1:T(8,128)}, u32[]{:S(2)}) copy-start(f32[8192,16]{0,1:T(8,128)} %get-tuple-element.204) | copy-start | bytes 1572868 | tf_op jit(solution)/shard_map/cond
  21.7 10.2 %copy-start.19 = (f32[8192,4]{0,1:T(4,128)S(1)}, f32[8192,4]{0,1:T(4,128)}, u32[]{:S(2)}) copy-start(f32[8192,4]{0,1:T(4,128)} %get-tuple-element.205) | copy-start | bytes 393220 | tf_op jit(solution)/shard_map/cond
  21.8 10.2 %copy-start.25 = (bf16[4,8,2048]{2,1,0:T(8,128)(2,1)S(1)}, bf16[4,8,2048]{2,1,0:T(8,128)(2,1)}, u32[]{:S(2)}) copy-start(bf16[4,8,2048]{2,1,0:T(8,128)(2,1)} %get-tuple-element.197.x) | copy-start | bytes 393220 | tf_op jit(solution)/shard_map/cond
  21.8 10.2 %copy-start.31 = (bf16[4,8,2048]{2,1,0:T(8,128)(2,1)S(1)}, bf16[4,8,2048]{2,1,0:T(8,128)(2,1)}, u32[]{:S(2)}) copy-start(bf16[4,8,2048]{2,1,0:T(8,128)(2,1)} %get-tuple-element.198.z) | copy-start | bytes 393220 | tf_op jit(solution)/shard_map/cond
  21.8 10.2 %copy-start.37 = (bf16[4,8,2048]{2,1,0:T(8,128)(2,1)S(1)}, bf16[4,8,2048]{2,1,0:T(8,128)(2,1)}, u32[]{:S(2)}) copy-start(bf16[4,8,2048]{2,1,0:T(8,128)(2,1)} %get-tuple-element.199.dt) | copy-start | bytes 393220 | tf_op jit(solution)/shard_map/cond
  25.2 24.0 %collective-permute-start.1 = (bf16[144,4096]{1,0:T(8,128)(2,1)}, bf16[144,4096]{1,0:T(8,128)(2,1)}, u32[]{:S(2)}, u32[]{:S(2)}) collective-permute-start(bf16[144,4096]{1,0:T(8,128)(2,1)} %get-tuple-element.427), channel_id=1, source_target_pairs={{4,8},{8,4},{5,9},{9,5},{6,10},{10,6},{7,11},{11,7},{20,24},{24,20... | collective-permute-start | bytes 3538952 | tf_op jit(solution)/shard_map/cond/branch_0_fun/ppermute | solution.py:419
  29.6 42.3 %collective-permute-start = (bf16[144,4096]{1,0:T(8,128)(2,1)}, bf16[144,4096]{1,0:T(8,128)(2,1)}, u32[]{:S(2)}, u32[]{:S(2)}) collective-permute-start(bf16[144,4096]{1,0:T(8,128)(2,1)} %get-tuple-element.428), channel_id=1, source_target_pairs={{4,8},{8,4},{5,9},{9,5},{6,10},{10,6},{7,11},{11,7},{20,24},{24,20... | collective-permute-start | bytes 3538952 | tf_op jit(solution)/shard_map/cond/branch_0_fun/ppermute | solution.py:419
  49.3 17.8 %collective-permute-start.2 = (bf16[144,4096]{1,0:T(8,128)(2,1)}, bf16[144,4096]{1,0:T(8,128)(2,1)S(1)}, u32[]{:S(2)}, u32[]{:S(2)}) collective-permute-start(bf16[144,4096]{1,0:T(8,128)(2,1)} %collective-permute-done.1.refs_0_), channel_id=1, source_target_pairs={{4,5},{8,9},{5,4},{9,8},{6,7},{10,11},{7,6},{11,10},{20,21},{24,25... | collective-permute-start | bytes 3538952 | tf_op jit(solution)/shard_map/cond/branch_0_fun/ppermute | solution.py:419
  53.3 17.5 %collective-permute-start.4 = (bf16[144,4096]{1,0:T(8,128)(2,1)}, bf16[144,4096]{1,0:T(8,128)(2,1)}, u32[]{:S(2)}, u32[]{:S(2)}) collective-permute-start(bf16[144,4096]{1,0:T(8,128)(2,1)} %collective-permute-done.1.refs_0_), channel_id=1, source_target_pairs={{4,20},{8,24},{5,21},{9,25},{6,22},{10,26},{7,23},{11,27},{20,4},{... | collective-permute-start | bytes 3538952 | tf_op jit(solution)/shard_map/cond/branch_0_fun/ppermute | solution.py:419
  56.4 2.6 collective-permute-start.10
  59.1 21.3 %collective-permute-start.8 = (bf16[160,896]{1,0:T(8,128)(2,1)S(1)}, bf16[160,896]{1,0:T(8,128)(2,1)S(1)}, u32[]{:S(2)}, u32[]{:S(2)}) collective-permute-start(bf16[160,896]{1,0:T(8,128)(2,1)S(1)} %constant_dynamic-slice_fusion.2), channel_id=1, source_target_pairs={{4,0},{8,12},{5,1},{9,13},{6,2},{10,14},{7,3},{11,15},{20,16},{24,... | collective-permute-start | bytes 860168 | tf_op jit(solution)/shard_map/cond/branch_0_fun/ppermute | solution.py:419
  67.1 8.2 %copy-start.45 = (bf16[144,4096]{1,0:T(8,128)(2,1)}, bf16[144,4096]{1,0:T(8,128)(2,1)S(1)}, u32[]{:S(2)}) copy-start(bf16[144,4096]{1,0:T(8,128)(2,1)S(1)} %collective-permute-done.2.refs_2_) | copy-start | bytes 3538948 | tf_op jit(solution)/shard_map/cond
  67.1 18.0 %collective-permute-start.11 = (bf16[32,2048]{1,0:T(8,128)(2,1)S(1)}, bf16[32,2048]{1,0:T(8,128)(2,1)S(1)}, u32[]{:S(2)}, u32[]{:S(2)}) collective-permute-start(bf16[32,2048]{1,0:T(8,128)(2,1)S(1)} %add_convert_fusion.1), channel_id=1, source_target_pairs={{0,8},{4,12},{8,0},{12,4},{1,9},{5,13},{9,1},{13,5},{2,10},{6,14},... | collective-permute-start | bytes 393224 | tf_op jit(solution)/shard_map/cond/branch_0_fun/ppermute | solution.py:419
  71.8 32.7 %copy-start.60 = (s32[11]{0:T(128)S(1)}, s32[11]{0:T(128)}, u32[]{:S(2)}) copy-start(s32[11]{0:T(128)} %get-tuple-element.193.sc) | copy-start | bytes 136 | tf_op jit(solution)/shard_map/cond
  75.3 143.2 %collective-permute-start.3 = (bf16[208,4096]{1,0:T(8,128)(2,1)}, bf16[208,4096]{1,0:T(8,128)(2,1)S(1)}, u32[]{:S(2)}, u32[]{:S(2)}) collective-permute-start(bf16[208,4096]{1,0:T(8,128)(2,1)} %get-tuple-element.430), channel_id=1, source_target_pairs={{4,20},{8,24},{5,21},{9,25},{6,22},{10,26},{7,23},{11,27},{20,4},{... | collective-permute-start | bytes 5111816 | tf_op jit(solution)/shard_map/cond/branch_0_fun/ppermute | solution.py:419
  78.4 140.1 %collective-permute-start.5 = (bf16[208,4096]{1,0:T(8,128)(2,1)}, bf16[208,4096]{1,0:T(8,128)(2,1)}, u32[]{:S(2)}, u32[]{:S(2)}) collective-permute-start(bf16[208,4096]{1,0:T(8,128)(2,1)} %get-tuple-element.429), channel_id=1, source_target_pairs={{4,5},{8,9},{5,4},{9,8},{6,7},{10,11},{7,6},{11,10},{20,21},{24,25... | collective-permute-start | bytes 5111816 | tf_op jit(solution)/shard_map/cond/branch_0_fun/ppermute | solution.py:419
  80.4 138.1 %collective-permute-start.6 = (bf16[160,4096]{1,0:T(8,128)(2,1)}, bf16[160,4096]{1,0:T(8,128)(2,1)}, u32[]{:S(2)}, u32[]{:S(2)}) collective-permute-start(bf16[160,4096]{1,0:T(8,128)(2,1)} %constant_dynamic-slice_fusion.4), channel_id=1, source_target_pairs={{4,8},{8,4},{5,9},{9,5},{6,10},{10,6},{7,11},{11,7},{20,24},{24,20... | collective-permute-start | bytes 3932168 | tf_op jit(solution)/shard_map/cond/branch_0_fun/ppermute | solution.py:419
  85.1 19.4 %collective-permute-start.9 = (bf16[160,1152]{1,0:T(8,128)(2,1)S(1)}, bf16[160,1152]{1,0:T(8,128)(2,1)S(1)}, u32[]{:S(2)}, u32[]{:S(2)}) collective-permute-start(bf16[160,1152]{1,0:T(8,128)(2,1)S(1)} %constant_dynamic-slice_fusion.1), channel_id=1, source_target_pairs={{4,8},{8,4},{5,9},{9,5},{6,10},{10,6},{7,11},{11,7},{20,24},{24,20... | collective-permute-start | bytes 1105928 | tf_op jit(solution)/shard_map/cond/branch_0_fun/ppermute | solution.py:419
  104.5 4.3 %collective-permute-start.12 = (bf16[32,2048]{1,0:T(8,128)(2,1)S(1)}, bf16[32,2048]{1,0:T(8,128)(2,1)S(1)}, u32[]{:S(2)}, u32[]{:S(2)}) collective-permute-start(bf16[32,2048]{1,0:T(8,128)(2,1)S(1)} %add_convert_fusion), channel_id=1, source_target_pairs={{0,4},{4,0},{8,12},{12,8},{1,5},{5,1},{9,13},{13,9},{2,6},{6,2},{1... | collective-permute-start | bytes 393224 | tf_op jit(solution)/shard_map/cond/branch_0_fun/ppermute | solution.py:419
  (1 other events, 1.2 us)
